TPU v7x, 32 devices: a whole 2x2x4 slice. The times are simulated.
32 devices in a mesh: grp: 2 (over x), sta: 16 (over z, y, core).
Axes of the slice: x: 2, y: 2, z: 4, core: 2. Of those that a mesh axis runs over, the one named last changes fastest.
Arguments:
- noise_window: float32 [1024, 4096], P(('grp', 'sta')), parts along dimension 0, may hold values from -6 to 6
- fir_taps: float32 [1024, 129], P(('grp', 'sta')), parts along dimension 0, may hold values from -0.5 to 0.5
- matchings: int32 [4, 16], replicated, may hold values from 0 to 15, each once within a row
- block_device: int32 [16], replicated, may hold values from 0 to 15, each once
Outputs:
- xcorr: float32 [4, 1024, 128], P(None, ('grp', 'sta')), parts along dimension 1
There are 2 independent parts, one for each index of `grp`. A program takes and returns all parts, laid end to end along the dimension named above; an argument that names none is the same for every part. Nothing has to cross between parts.
Inputs may be any that keep to these rules, and one draw needn't show every extreme that they name: Each row of matchings is a permutation of the 16 block numbers. block_device is a permutation of the 16 block numbers.
All inputs are finite; a program needn't handle non-finite values.
Results may differ from a plain program's by a relative error of at most 0.0027.
Values may be sent and summed in bfloat16 or wider, within the bound.
A program may use at most 64 MiB of HBM per device.

v0:
```python
import jax
import jax.numpy as jnp
from jax import lax
from jax.sharding import PartitionSpec as P

LAGS = 128


def passed_along(block, axis, distance):
    devices = range(lax.axis_size(axis))
    route = [(i - distance, i) for i in devices if i - distance in devices]
    return lax.ppermute(block, axis, route)


def whiten(signal, taps, lag_count):
    row_count, total = signal.shape
    tile_count = total // lag_count
    ntaps = taps.shape[1]
    tiles = signal.reshape(row_count, tile_count, lag_count)
    previous = jnp.concatenate(
        [jnp.zeros((row_count, 1, lag_count), jnp.float32), tiles[:, :-1]], axis=1
    )
    joined = jnp.concatenate([previous, tiles], axis=2)
    inner = jnp.arange(2 * lag_count, dtype=jnp.int32)[:, None]
    outer = jnp.arange(lag_count, dtype=jnp.int32)[None, :]
    offset = lag_count + outer - inner
    valid = (offset >= 0) & (offset < ntaps)
    position = jnp.where(valid, offset, ntaps)
    padded = jnp.concatenate([taps, jnp.zeros((row_count, 1), jnp.float32)], axis=1)
    table = padded[:, position]
    result = jnp.einsum("rkj,rjo->rko", joined, table, precision=lax.Precision.HIGHEST)
    return result.reshape(row_count, total)


def invert(perm):
    count = perm.shape[-1]
    numbers = jnp.arange(count, dtype=jnp.int32)
    equal = perm[..., :, None] == numbers
    return jnp.sum(jnp.where(equal, numbers[:, None], 0), axis=-2)


def lookup(table, index):
    count = table.shape[-1]
    numbers = jnp.arange(count, dtype=jnp.int32)
    equal = index[..., :, None] == numbers
    return jnp.sum(jnp.where(equal, table[..., None, :], 0), axis=-1)


def partner_rows(matchings, block_device, row_count):
    match_count, block_count = matchings.shape
    block_size = row_count // block_count
    owner_of = invert(block_device)
    inverse_match = invert(matchings)
    held = jnp.broadcast_to(block_device, (match_count, block_count))
    partner_dev = lookup(owner_of, lookup(matchings, held))
    source_dev = lookup(owner_of, lookup(inverse_match, held))
    rowids = jnp.arange(row_count, dtype=jnp.int32)
    device_of = jnp.broadcast_to(rowids // block_size, (match_count, row_count))
    within = rowids % block_size
    prow = lookup(partner_dev, device_of) * block_size + within
    qrow = lookup(source_dev, device_of) * block_size + within
    return (prow, qrow)


def correlate(extended, stacked, lag_count):
    row_count, match_count, seg_len = stacked.shape
    signal = extended[:, : seg_len + lag_count - 1].reshape(1, row_count, seg_len + lag_count - 1)
    kernels = stacked.reshape(row_count * match_count, 1, seg_len)
    result = lax.conv_general_dilated(
        signal,
        kernels,
        (1,),
        "VALID",
        dimension_numbers=("NCH", "OIH", "NCH"),
        feature_group_count=row_count,
        preferred_element_type=jnp.float32,
    )
    return result.reshape(row_count * match_count, lag_count)


def per_device(noise_window, fir_taps, matchings, block_device):
    row_count, total = noise_window.shape
    blocks = lax.axis_size("sta")
    stations = row_count * blocks
    whitened = whiten(noise_window, fir_taps, LAGS)
    squashed = (whitened / (1.0 + jnp.abs(whitened))).astype(jnp.bfloat16)
    local = lax.all_to_all(squashed, "sta", split_axis=1, concat_axis=0, tiled=True)
    following = passed_along(local[:, :LAGS], "sta", -1)
    extended = jnp.concatenate([local, following], axis=1)
    prow, qrow = partner_rows(matchings, block_device, stations)
    match_count = matchings.shape[0]
    stacked = jnp.take(local, qrow.T, axis=0)
    result = correlate(extended, stacked, LAGS)
    flat_index = prow * match_count + jnp.arange(match_count, dtype=jnp.int32)[:, None]
    partial_sums = jnp.take(result, flat_index, axis=0)
    owned = lax.psum_scatter(partial_sums, "sta", scatter_dimension=1, tiled=True)
    return owned / jnp.sqrt(jnp.float32(total))


def solution(mesh):
    return jax.shard_map(
        per_device,
        mesh=mesh,
        in_specs=(P(("grp", "sta"), None), P(("grp", "sta"), None), P(), P()),
        out_specs=P(None, ("grp", "sta"), None),
        check_vma=False,
    )
```

profile of v0, /device:TPU:0, one launch (start us, length us, event | category | flops | bytes accessed | tf_op | source)
XLA Modules:
  0.0 272.8 jit_solution(3465383660032516592)
XLA Ops:
  6.5 0.9 copy.27
  7.4 0.1 fusion.10
  7.5 108.2 %gather_fusion = f32[32768,32]{1,0:T(8,128)} fusion(f32[32,130]{0,1:T(8,128)S(1)} %concatenate.14, s32[32768]{0:T(1024)S(1)} %fusion.10), kind=kCustom, calls=%fused_computation | custom fusion | bytes 8519680 | tf_op jit(solution)/shard_map/gather | solution.py:30
  115.7 0.0 copy-start
  115.7 11.8 %copy.28 = f32[256,128,32]{1,0,2:T(8,128)} copy(f32[256,128,32]{2,1,0:T(8,128)} %bitcast.39) | data formatting | bytes 8388608 | tf_op jit(solution)/shard_map/gather | solution.py:30
  127.4 0.0 copy-done
  127.5 0.1 copy.35
  127.5 0.0 copy-start.2
  127.6 0.0 copy-start.1
  127.6 4.2 %fusion = f32[32,32,128]{2,1,0:T(8,128)S(1)} fusion(f32[256,128,32]{1,0,2:T(8,128)} %copy.28, f32[32,31,128]{2,1,0:T(8,128)S(1)} %bitcast.41, f32[32,32,128]{2,1,0:T(8,128)S(1)} %bitcast.40), kind=kOutput, calls=%fused_computation.3 | convolution fusion | flops 403439616 | bytes 5750784 | tf_op jit(solution)/shard_map/rkj,rjo->rko/dot_general | solution.py:31
  131.8 0.1 reshape.178
  131.9 1.0 divide_convert_fusion
  133.0 7.4 %all-to-all-start = ((bf16[32,16,256]{2,0,1:T(8,128)(2,1)}), bf16[32,16,256]{2,0,1:T(8,128)(2,1)S(1)}, u32[]{:S(2)}, u32[]{:S(2)}) async-start(bf16[32,16,256]{2,0,1:T(8,128)(2,1)} %divide_convert_fusion), calls=%async_computation | async-start | bytes 524288 | tf_op jit(solution)/shard_map/all_to_all | solution.py:87
  140.4 0.0 reduce-scatter.2.cloned.1.call-start
  140.4 0.0 copy-done.2
  140.4 0.1 select_reduce_fusion.7
  140.5 0.0 copy-done.1
  140.5 0.2 select_reduce_fusion.6
  140.7 0.2 select_reduce_fusion.3
  141.0 0.3 select_reduce_fusion.5
  141.3 0.1 select_reduce_fusion.1
  141.4 0.1 copy.31
  141.6 0.2 reshape.191
  141.8 8.6 %all-to-all-done = bf16[32,16,256]{2,0,1:T(8,128)(2,1)S(1)} async-done(((bf16[32,16,256]{2,0,1:T(8,128)(2,1)}), bf16[32,16,256]{2,0,1:T(8,128)(2,1)S(1)}, u32[]{:S(2)}, u32[]{:S(2)}) %all-to-all-start) | async-done | bytes 262176 | tf_op jit(solution)/shard_map/all_to_all | solution.py:87
  150.4 1.3 collective-permute-start
  151.7 7.5 %gather_fusion.1 = bf16[2048,256]{1,0:T(8,128)(2,1)S(1)} fusion(bf16[512,256]{1,0:T(8,128)(2,1)S(1)} %bitcast.36, s32[2048]{0:T(1024)S(1)} %broadcast_clamp_fusion.1), kind=kCustom, calls=%fused_computation.1 | custom fusion | bytes 2105344 | tf_op jit(solution)/shard_map/jit(_take)/gather | solution.py:92
  159.2 0.3 gather.15
  159.5 4.1 %copy.32 = bf16[512,4,1,256]{0,2,1,3:T(2,128)(2,1)} copy(bf16[512,4,1,256]{3,1,0,2:T(4,128)(2,1)S(1)} %gather.15) | data formatting | bytes 2097152 | tf_op jit(solution)/shard_map/jit(_take)/gather | solution.py:92
  163.7 0.0 collective-permute-done
  163.7 1.1 copy.33
  164.9 34.1 %fusion.2 = f32[1,512,4,128]{1,0,2,3:T(1,128)S(1)} fusion(bf16[1,512,383,1]{1,0,3,2:T(2,128)(2,1)S(1)} %copy.33, bf16[512,4,1,256]{0,2,1,3:T(2,128)(2,1)} %copy.32, pred[512,4]{0,1:T(4,128)(4,1)S(1)} %get-tuple-element.11), kind=kOutput, calls=%fused_computation.6 | convolution fusion | flops 134742016 | bytes 2491392 | tf_op jit(solution)/shard_map/convolution
  199.0 1.4 copy.34
  200.4 5.5 %gather_fusion.2 = f32[2048,128]{1,0:T(8,128)S(1)} fusion(f32[2048,128]{1,0:T(8,128)S(1)} %bitcast.38, s32[2048]{0:T(1024)S(1)} %broadcast_clamp_fusion), kind=kCustom, calls=%fused_computation.2 | custom fusion | bytes 2105344 | tf_op jit(solution)/shard_map/jit(_take)/gather | solution.py:95
  205.8 1.3 broadcast_select_fusion.2
  207.2 0.0 reduce-scatter.2.cloned.1.call-update
  207.2 57.3 %reduce-scatter.2.cloned.1.call-done = f32[4,32,128]{2,1,0:T(8,128)} async-done(((f32[4,512,128]{2,1,0:T(8,128)}), f32[4,32,128]{2,1,0:T(8,128)}) %reduce-scatter.2.cloned.1.call-update) | async-done | bytes 65552 | tf_op jit(solution)/shard_map/reduce_scatter | solution.py:96
  264.5 1.5 broadcast_multiply_fusion
  (12 shorter events, 0.1 us)
Async XLA Ops:
  115.7 11.8 %copy-start = (f32[32,4096]{1,0:T(8,128)S(1)}, f32[32,4096]{1,0:T(8,128)}, u32[]{:S(2)}) copy-start(f32[32,4096]{1,0:T(8,128)} %param.4) | copy-start | bytes 1572868
  127.5 12.9 %copy-start.2 = (s32[16]{0:T(128)S(1)}, s32[16]{0:T(128)}, u32[]{:S(2)}) copy-start(s32[16]{0:T(128)} %param.7) | copy-start | bytes 196
  127.6 13.0 %copy-start.1 = (s32[4,16]{1,0:T(4,128)S(1)}, s32[4,16]{1,0:T(4,128)}, u32[]{:S(2)}) copy-start(s32[4,16]{1,0:T(4,128)} %param.6) | copy-start | bytes 772
  133.0 17.4 %all-to-all-start = ((bf16[32,16,256]{2,0,1:T(8,128)(2,1)}), bf16[32,16,256]{2,0,1:T(8,128)(2,1)S(1)}, u32[]{:S(2)}, u32[]{:S(2)}) async-start(bf16[32,16,256]{2,0,1:T(8,128)(2,1)} %divide_convert_fusion), calls=%async_computation | async-start | bytes 524288 | tf_op jit(solution)/shard_map/all_to_all | solution.py:87
  140.4 124.1 %reduce-scatter.2.cloned.1.call-start = ((), (), s32[]{:S(2)}) async-start(), calls=%async_computation.2 | async-start | bytes 1114112 | tf_op jit(solution)/shard_map/reduce_scatter | solution.py:96
  150.4 13.3 %collective-permute-start = (bf16[512,128]{1,0:T(8,128)(2,1)S(1)}, bf16[512,128]{1,0:T(8,128)(2,1)S(1)}, u32[]{:S(2)}, u32[]{:S(2)}) collective-permute-start(bf16[512,128]{1,0:T(8,128)(2,1)S(1)} %slice.19), channel_id=1, source_target_pairs={{1,0},{2,1},{3,2},{4,3},{5,4},{6,5},{7,6},{8,7},{9,8},{10,9},{11,1... | collective-permute-start | bytes 393224 | tf_op jit(solution)/shard_map/ppermute | solution.py:12
Sparse Core Ops, SparseCore 0:
  207.3 57.1 reduce-scatter.1
where the time goes:
time: 273 us
  local copies, waits for them, and re-layouts  141 us (52%)
  waiting for transfers between devices  65.9 us (24%)
  matrix products  38.3 us (14%)
  between operations  13.6 us (5%)
  starting transfers between devices  8.72 us (3%)
  other arithmetic  4.94 us (2%)
    gather x2, local copies, waits for them, and re-layouts, whiten(): table = padded[:, position]  120 us
    reduce_scatter x1, waiting for transfers between devices, per_device(): lax.psum_scatter(partial_sums, 'sta', scatter_dimension=1, tiled=True)  57.3 us
    another operation x1, matrix products  34.1 us
    gather x3, local copies, waits for them, and re-layouts, per_device(): stacked = jnp.take(local, qrow.T, axis=0)  11.9 us
    all_to_all x1, waiting for transfers between devices, per_device(): lax.all_to_all(squashed, 'sta', split_axis=1, concat_axis=0, tiled=True)  8.61 us
    all_to_all x1, starting transfers between devices, per_device(): lax.all_to_all(squashed, 'sta', split_axis=1, concat_axis=0, tiled=True)  7.39 us
    gather x1, local copies, waits for them, and re-layouts, per_device(): partial_sums = jnp.take(result, flat_index, axis=0)  5.46 us
  transfers between devices with their start and end apart: 3, of which 2 were waited for; matrix products, arithmetic and copies ran while one was open for 5% of the time, Pallas kernels for 0%

commit v1 on v0

v1 whole, which is shorter than its diff:
```python
import functools

import jax
import jax.numpy as jnp
from jax import lax
from jax.experimental import pallas as pl
from jax.experimental.pallas import tpu as pltpu
from jax.sharding import PartitionSpec as P

LAGS = 128
F32 = jnp.float32
BF16 = jnp.bfloat16


def split_bf16(x):
    high = x.astype(BF16)
    low = (x - high.astype(F32)).astype(BF16)
    return high, low


def whiten_kernel(x_ref, taps_ref, sq_ref, rev_ref, prev_ref, xs_ref, ys_ref):
    rows, total = x_ref.shape
    tiles = total // LAGS
    pitch = tiles + 8
    zeros8 = jnp.zeros((8, LAGS), F32)
    for r in range(rows):
        xs_ref[pl.ds(r * pitch, 8), :] = zeros8
    for n in range(tiles):
        xs_ref[pl.ds(8 + n, rows, stride=pitch), :] = x_ref[:, n * LAGS:(n + 1) * LAGS]
    ys_ref[pl.ds(0, 8), :] = zeros8
    row_id = lax.broadcasted_iota(jnp.int32, (LAGS, LAGS), 0)
    col_id = lax.broadcasted_iota(jnp.int32, (LAGS, LAGS), 1)

    mirror = jnp.where(row_id + col_id == LAGS - 1, 1.0, 0.0).astype(BF16)

    def one_row(r, carry):
        base = pl.multiple_of(r * pitch, 8)
        cur = xs_ref[pl.ds(base + 8, tiles), :]
        before = xs_ref[pl.ds(base + 7, tiles), :]
        joined = jnp.concatenate([before, cur], axis=1)
        tap = taps_ref[pl.ds(r, 1), :]
        spread = jnp.broadcast_to(tap[:, :LAGS], (LAGS, LAGS))
        rolled = pltpu.roll(spread, 0, 1, stride=1, stride_axis=0)
        last = jnp.broadcast_to(tap[:, LAGS:LAGS + 1], (LAGS, LAGS))
        cur_t = jnp.where(col_id >= row_id, rolled, 0.0)
        prev_t = jnp.where(col_id < row_id, rolled, jnp.where(col_id == row_id, last, 0.0))
        table = jnp.concatenate([prev_t, cur_t], axis=0)
        xh, xl = split_bf16(joined)
        th, tl = split_bf16(table)
        dot = functools.partial(jnp.dot, preferred_element_type=F32)
        white = dot(xh, th) + (dot(xh, tl) + dot(xl, th))
        squashed = white / (1.0 + jnp.abs(white))
        ys_ref[pl.ds(8, tiles), :] = squashed
        shifted = ys_ref[pl.ds(7, tiles), :]
        out = pl.multiple_of(r * tiles, 16)
        rounded = squashed.astype(BF16)
        sq_ref[pl.ds(out, tiles), :] = rounded
        rev_ref[pl.ds(out, tiles), :] = dot(rounded, mirror).astype(BF16)
        prev_ref[pl.ds(out, tiles), :] = dot(shifted.astype(BF16), mirror).astype(BF16)
        return carry

    lax.fori_loop(0, rows, one_row, 0)


def whiten(noise, taps):
    rows, total = noise.shape
    tiles = total // LAGS
    shape = jax.ShapeDtypeStruct((rows * tiles, LAGS), BF16)
    return pl.pallas_call(
        whiten_kernel,
        out_shape=[shape] * 3,
        in_specs=[pl.BlockSpec(memory_space=pltpu.VMEM)] * 2,
        out_specs=[pl.BlockSpec(memory_space=pltpu.VMEM)] * 3,
        scratch_shapes=[
            pltpu.VMEM((rows * (tiles + 8), LAGS), F32),
            pltpu.VMEM((tiles + 8, LAGS), F32),
        ],
        compiler_params=pltpu.CompilerParams(vmem_limit_bytes=48 * 2**20),
    )(noise, taps)


def correlate_kernel(matchings_ref, device_ref, rev_ref, prev_ref, all_ref, out_ref, held, sems):
    matches, blocks = matchings_ref.shape
    rows = out_ref.shape[1]
    tiles = rev_ref.shape[0] // rows
    size = rows * tiles
    me = lax.axis_index("sta")
    mine = device_ref[me]
    copies = []
    for m in range(matches):
        wanted = matchings_ref[m, mine]
        partner = jnp.int32(0)
        for e in range(blocks):
            partner = jnp.where(device_ref[e] == wanted, e, partner)
        start = pl.multiple_of(partner * size, 16)
        copy = pltpu.make_async_copy(all_ref.at[pl.ds(start, size), :], held.at[m], sems.at[m])
        copy.start()
        copies.append(copy)
    for copy in copies:
        copy.wait()
    row_id = lax.broadcasted_iota(jnp.int32, (LAGS, LAGS), 0)
    col_id = lax.broadcasted_iota(jnp.int32, (LAGS, LAGS), 1)
    upper = col_id + row_id >= LAGS - 1
    scale = 1.0 / (tiles * LAGS) ** 0.5

    def one_row(r, carry):
        at = pl.multiple_of(r * tiles, 16)
        left = jnp.concatenate([rev_ref[pl.ds(at, tiles), :], prev_ref[pl.ds(at, tiles), :]], axis=1)
        for m in range(matches):
            right = held[m, pl.ds(at, tiles), :]
            gram = lax.dot_general(left, right, (((0,), (0,)), ((), ())), preferred_element_type=F32)
            chosen = jnp.where(upper, gram[:LAGS], gram[LAGS:])
            turned = pltpu.roll(chosen, 1, 1, stride=1, stride_axis=0)
            out_ref[m, pl.ds(r, 1), :] = jnp.sum(turned, axis=0, keepdims=True) * scale
        return carry

    lax.fori_loop(0, rows, one_row, 0)


def correlate(matchings, block_device, rev, prev, gathered, rows):
    matches = matchings.shape[0]
    return pl.pallas_call(
        correlate_kernel,
        out_shape=jax.ShapeDtypeStruct((matches, rows, LAGS), F32),
        in_specs=[pl.BlockSpec(memory_space=pltpu.SMEM)] * 2
        + [pl.BlockSpec(memory_space=pltpu.VMEM)] * 2
        + [pl.BlockSpec(memory_space=pl.ANY)],
        out_specs=pl.BlockSpec(memory_space=pltpu.VMEM),
        scratch_shapes=[
            pltpu.VMEM((matches,) + rev.shape, BF16),
            pltpu.SemaphoreType.DMA((matches,)),
        ],
        compiler_params=pltpu.CompilerParams(vmem_limit_bytes=48 * 2**20),
    )(matchings, block_device, rev, prev, gathered)


def per_device(noise_window, fir_taps, matchings, block_device):
    rows = noise_window.shape[0]
    sq, rev, prev = whiten(noise_window, fir_taps)
    gathered = lax.all_gather(sq, "sta", axis=0, tiled=True)
    return correlate(matchings, block_device, rev, prev, gathered, rows)


def solution(mesh):
    return jax.shard_map(
        per_device,
        mesh=mesh,
        in_specs=(P(("grp", "sta"), None), P(("grp", "sta"), None), P(), P()),
        out_specs=P(None, ("grp", "sta"), None),
        check_vma=False,
    )
```

time: 273 us -> 97.7 us (0.36)
  local copies, waits for them, and re-layouts: 141 us -> 5.32 us
  matrix products: 38.3 us -> 0 us
  Pallas kernels: 0 us -> 25.2 us
  waiting for transfers between devices: 65.9 us -> 53.4 us
  starting transfers between devices: 8.72 us -> 0.01 us
  other arithmetic: 4.94 us -> 0 us
    gather x6 -> x0, local copies, waits for them, and re-layouts: 137 us -> none  [the longest x2 120 us: whiten(): table = padded[:, position]]
    reduce_scatter x1 -> x0, waiting for transfers between devices: 57.3 us -> none  [per_device(): lax.psum_scatter(partial_sums, 'sta', scatter_dimension=1, tiled=True)]
    all_gather x0 -> x1, waiting for transfers between devices: none -> 53.4 us  [per_device(): gathered = lax.all_gather(sq, 'sta', axis=0, tiled=True)]
    another operation x1 -> x0, matrix products: 34.1 us -> none
    pallas_call x0 -> x2, Pallas kernels: none -> 25.2 us  [the longest x1 12.8 us: whiten(): pl.pallas_call(whiten_kernel, out_shape=[shape] * 3, in_specs=[pl.BlockSp...]
    all_to_all x1 -> x0, waiting for transfers between devices: 8.61 us -> none  [per_device(): lax.all_to_all(squashed, 'sta', split_axis=1, concat_axis=0, tiled=True)]
    all_to_all x1 -> x0, starting transfers between devices: 7.39 us -> none  [per_device(): lax.all_to_all(squashed, 'sta', split_axis=1, concat_axis=0, tiled=True)]
    unnamed x9 -> x10, local copies, waits for them, and re-layouts: 0.97 us -> 5.32 us
  transfers between devices with their start and end apart: 3 -> 1, of which waited for: 2 -> 1; matrix products, arithmetic and copies ran while one was open for 5% -> 0% of each run, Pallas kernels for 0% -> 0%
where the time goes in v1:
time: 97.7 us; the launch traced here: 97.4 us
  waiting for transfers between devices  53.4 us (55%)
  Pallas kernels  25.2 us (26%)
  between operations  13.4 us (14%)
  local copies, waits for them, and re-layouts  5.32 us (5%)
    all_gather x1, waiting for transfers between devices, per_device(): gathered = lax.all_gather(sq, 'sta', axis=0, tiled=True)  53.4 us
    pallas_call x1, Pallas kernels, whiten(): pl.pallas_call(whiten_kernel, out_shape=[shape] * 3, in_specs=[pl.BlockSp...  12.8 us
    pallas_call x1, Pallas kernels, correlate(): pl.pallas_call(correlate_kernel, out_shape=jax.ShapeDtypeStruct((matches,...  12.4 us
    unnamed x10, local copies, waits for them, and re-layouts  5.32 us
  transfers between devices with their start and end apart: 1, of which 1 were waited for; matrix products, arithmetic and copies ran while one was open for 0% of the time, Pallas kernels for 0%

profile of v1, /device:TPU:0, one launch (start us, length us, event | category | flops | bytes accessed | tf_op | source)
XLA Modules:
  0.0 97.4 jit_solution(11945512811833012646)
XLA Ops:
  6.5 0.0 all-gather.2.cloned.1.call-start
  6.5 0.0 copy-start.1
  6.5 1.0 %copy-done.1 = f32[32,4096]{1,0:T(8,128)S(1)} copy-done((f32[32,4096]{1,0:T(8,128)S(1)}, f32[32,4096]{1,0:T(8,128)}, u32[]{:S(2)}) %copy-start.1) | copy-done | bytes 524312
  7.6 0.0 copy-start.2
  7.6 0.8 copy-done.2
  8.3 12.8 %shard_map.46 = (bf16[1024,128]{1,0:T(8,128)(2,1)}, bf16[1024,128]{1,0:T(8,128)(2,1)S(1)}, bf16[1024,128]{1,0:T(8,128)(2,1)S(1)}) custom-call(f32[32,4096]{1,0:T(8,128)S(1)} %copy-done.1, f32[32,129]{1,0:T(8,128)S(1)} %copy-done.2), custom_call_target="tpu_custom_call" | custom-call | tf_op jit(solution)/shard_map/pallas_call | solution.py:69
  21.1 0.0 all-gather.2.cloned.1.call-update
  21.2 53.4 %all-gather.2.cloned.1.call-done.all_ref = bf16[16384,128]{1,0:T(8,128)(2,1)} async-done(((bf16[1024,128]{1,0:T(8,128)(2,1)}), bf16[16384,128]{1,0:T(8,128)(2,1)}) %all-gather.2.cloned.1.call-update) | async-done | bytes 4194320 | tf_op jit(solution)/shard_map/all_gather | solution.py:140
  74.6 0.0 copy-start
  74.6 2.2 %copy-done = bf16[16384,128]{1,0:T(8,128)(2,1)S(1)} copy-done((bf16[16384,128]{1,0:T(8,128)(2,1)S(1)}, bf16[16384,128]{1,0:T(8,128)(2,1)}, u32[]{:S(2)}) %copy-start) | copy-done | bytes 4194328
  76.8 0.0 copy-start.3
  76.8 0.7 copy-done.3
  77.4 0.0 copy-start.4
  77.5 0.7 copy-done.4
  78.1 12.4 %shard_map.47 = f32[4,32,128]{2,1,0:T(8,128)} custom-call(s32[4,16]{1,0:T(4,128)S(1)} %copy-done.3, s32[16]{0:T(128)S(1)} %copy-done.4, bf16[1024,128]{1,0:T(8,128)(2,1)S(1)} %get-tuple-element.8.rev_ref, bf16[1024,128]{1,0:T(8,128)(2,1)S(1)} %get-tuple-element.9.prev_ref, bf16[16384,128]{1,0:T(8,128)(2,1)S(1)} %copy-done), custom_call_target="tpu_custom_call" | custom-call | tf_op jit(solution)/shard_map/pallas_call | solution.py:122
Async XLA Ops:
  6.5 68.0 %all-gather.2.cloned.1.call-start = ((), (), s32[]{:S(2)}) async-start(), calls=%async_computation | async-start | bytes 4456448 | tf_op jit(solution)/shard_map/all_gather | solution.py:140
  6.5 1.0 %copy-start.1 = (f32[32,4096]{1,0:T(8,128)S(1)}, f32[32,4096]{1,0:T(8,128)}, u32[]{:S(2)}) copy-start(f32[32,4096]{1,0:T(8,128)} %x_ref.1) | copy-start | bytes 1572868
  7.6 0.8 copy-start.2
  74.6 2.2 %copy-start = (bf16[16384,128]{1,0:T(8,128)(2,1)S(1)}, bf16[16384,128]{1,0:T(8,128)(2,1)}, u32[]{:S(2)}) copy-start(bf16[16384,128]{1,0:T(8,128)(2,1)} %all-gather.2.cloned.1.call-done.all_ref) | copy-start | bytes 12582916
  76.8 0.7 copy-start.3
  77.4 0.7 copy-start.4
Sparse Core Ops, SparseCore 0:
  21.3 53.2 all-gather.1

commit v2 on v0

v2 whole, which is shorter than its diff:
```python
import functools

import jax
import jax.numpy as jnp
from jax import lax
from jax.experimental import pallas as pl
from jax.experimental.pallas import tpu as pltpu
from jax.sharding import PartitionSpec as P

LAGS = 128
F32 = jnp.float32
BF16 = jnp.bfloat16
SIB, ACROSS, DOWN, UP = range(4)


def split_bf16(x):
    high = x.astype(BF16)
    low = (x - high.astype(F32)).astype(BF16)
    return high, low


def kernel(width, part, noise_ref, taps_ref, matchings_ref, device_ref, out_ref,
           noise, taps, matchings, device, xs, ys, gathered, before, acc,
           in_sems, send_sems, recv_sems):
    blocks, parts, chunk, _ = gathered.shape
    rows, total = noise.shape
    matches = matchings.shape[0]
    tiles = total // LAGS
    pitch = tiles + 8
    me = lax.axis_index("sta")
    depth = blocks // (2 * width)
    core = me % 2
    y = (me // 2) % width
    z = me // (2 * width)
    sibling = me + 1 - 2 * core
    across = me + 2 - 4 * y
    down, up = me - 2 * width, me + 2 * width
    has_down, has_up = z > 0, z < depth - 1

    loads = [
        pltpu.make_async_copy(taps_ref, taps, in_sems.at[0]),
        pltpu.make_async_copy(matchings_ref, matchings, in_sems.at[1]),
        pltpu.make_async_copy(device_ref, device, in_sems.at[2]),
    ]

    def noise_load(k):
        span = pl.ds(pl.multiple_of(k * part, 8), part)
        return pltpu.make_async_copy(noise_ref.at[span, :], noise.at[span, :], in_sems.at[3 + k])

    noise_load(0).start()
    for load in loads:
        load.start()
    for k in range(1, parts):
        noise_load(k).start()

    barrier = pltpu.get_barrier_semaphore()
    greet = functools.partial(pl.semaphore_signal, barrier, inc=1)
    greet(device_id={"sta": sibling})
    if width > 1:
        greet(device_id={"sta": across})

    @pl.when(has_down)
    def _():
        greet(device_id={"sta": down})

    @pl.when(has_up)
    def _():
        greet(device_id={"sta": up})

    def copy(block, k, way, target):
        return pltpu.make_async_remote_copy(
            src_ref=gathered.at[block, k],
            dst_ref=gathered.at[block, k],
            send_sem=send_sems.at[way, block, k],
            recv_sem=recv_sems.at[block, k],
            device_id={"sta": target},
        )

    def landed(block, k):
        copy(block, k, SIB, sibling).wait_recv()

    row_id = lax.broadcasted_iota(jnp.int32, (LAGS, LAGS), 0)
    col_id = lax.broadcasted_iota(jnp.int32, (LAGS, LAGS), 1)
    upper = col_id >= row_id

    zeros8 = jnp.zeros((8, LAGS), F32)
    for r in range(part):
        xs[pl.ds(r * pitch, 8), :] = zeros8
        ys[pl.ds(r * pitch, 8), :] = zeros8
    for load in loads:
        load.wait()

    def whiten_part(k, carry):
        noise_load(k).wait()
        span = pl.ds(pl.multiple_of(k * part, 8), part)
        for n in range(tiles):
            xs[pl.ds(8 + n, part, stride=pitch), :] = noise[span, n * LAGS:(n + 1) * LAGS]
        tap_rows = taps[span, :]
        for r in range(part):
            cur = xs[pl.ds(r * pitch + 8, tiles), :]
            prior = xs[pl.ds(r * pitch + 7, tiles), :]
            joined = jnp.concatenate([prior, cur], axis=1)
            tap = tap_rows[r:r + 1]
            spread = jnp.broadcast_to(tap[:, :LAGS], (LAGS, LAGS))
            rolled = pltpu.roll(spread, 0, 1, stride=1, stride_axis=0)
            last = jnp.broadcast_to(tap[:, LAGS:LAGS + 1], (LAGS, LAGS))
            cur_t = jnp.where(upper, rolled, 0.0)
            prior_t = jnp.where(upper, jnp.where(col_id == row_id, last, 0.0), rolled)
            table = jnp.concatenate([prior_t, cur_t], axis=0)
            left = jnp.concatenate(split_bf16(joined), axis=0)
            right = jnp.concatenate(split_bf16(table), axis=1)
            four = jnp.dot(left, right, preferred_element_type=F32)
            white = four[:tiles, :LAGS] + (four[tiles:, :LAGS] + four[:tiles, LAGS:] + four[tiles:, LAGS:])
            squashed = white / (1.0 + jnp.abs(white))
            ys[pl.ds(r * pitch + 8, tiles), :] = squashed
            gathered[me, k, pl.ds(r * tiles, tiles), :] = squashed.astype(BF16)
            shifted = ys[pl.ds(r * pitch + 7, tiles), :]
            before[k, pl.ds(r * tiles, tiles), :] = shifted.astype(BF16)

        @pl.when(k == 0)
        def _():
            pl.semaphore_wait(barrier, 1 + (width > 1) + has_down.astype(jnp.int32) + has_up.astype(jnp.int32))

        if width > 1:
            copy(me, k, ACROSS, across).start()

        @pl.when(has_down)
        def _():
            copy(me, k, DOWN, down).start()

        @pl.when(has_up)
        def _():
            copy(me, k, UP, up).start()

        copy(me, k, SIB, sibling).start()
        return carry

    lax.fori_loop(0, parts, whiten_part, 0)

    def along(z_of, way, target, onward, k):
        block = z_of * 2 * width + y * 2 + core
        landed(block, k)
        if width > 1:
            copy(block, k, ACROSS, across).start()

        @pl.when(onward)
        def _():
            copy(block, k, way, target).start()

        copy(block, k, SIB, sibling).start()

    def from_across(z_of, k):
        block = z_of * 2 * width + (1 - y) * 2 + core
        landed(block, k)
        copy(block, k, SIB, sibling).start()

    def round_part(i, carry):
        d = i // parts
        k = i % parts

        @pl.when((d > 0) & (z - d >= 0))
        def _():
            along(z - d, UP, up, has_up, k)

        @pl.when((d > 0) & (z + d < depth))
        def _():
            along(z + d, DOWN, down, has_down, k)

        if width > 1:
            @pl.when((d > 0) & (z - d + 1 >= 0))
            def _():
                from_across(z - d + 1, k)

            @pl.when((d > 1) & (z + d - 1 < depth))
            def _():
                from_across(z + d - 1, k)

        return carry

    lax.fori_loop(parts, (depth + 1) * parts, round_part, 0)

    def last_part(i, carry):
        pair = i // parts
        k = i % parts
        landed(2 * pair + 1 - core, k)
        return carry

    lax.fori_loop(0, blocks // 2 * parts, last_part, 0)

    partners = []
    mine = device[me]
    for m in range(matches):
        wanted = matchings[m, mine]
        partner = jnp.int32(0)
        for e in range(blocks):
            partner = jnp.where(device[e] == wanted, e, partner)
        partners.append(partner)

    def correlate_row(r, carry):
        k = r // part
        span = pl.ds(pl.multiple_of((r % part) * tiles, 16), tiles)
        left = jnp.concatenate([gathered[me, k, span, :], before[k, span, :]], axis=1)
        right = jnp.concatenate([gathered[partner, k, span, :] for partner in partners], axis=1)
        gram = lax.dot_general(left, right, (((0,), (0,)), ((), ())), preferred_element_type=F32)
        for m in range(matches):
            lanes = slice(m * LAGS, (m + 1) * LAGS)
            chosen = jnp.where(upper, gram[:LAGS, lanes], gram[LAGS:, lanes])
            terms = [chosen[:8]]
            for g in range(8, LAGS, 8):
                terms.append(pltpu.roll(chosen[g:g + 8], LAGS - g, 1))
            while len(terms) > 1:
                terms = [a + b for a, b in zip(terms[::2], terms[1::2])]
            acc[pl.ds(pl.multiple_of((m * rows + r) * 8, 8), 8), :] = terms[0]
        return carry

    lax.fori_loop(0, rows, correlate_row, 0, unroll=2)

    scale = 1.0 / total ** 0.5
    for m in range(matches):
        lags = acc[pl.ds(m * rows * 8, rows, stride=8), :]
        for s in range(1, 8):
            lags += pltpu.roll(acc[pl.ds(m * rows * 8 + s, rows, stride=8), :], LAGS - s, 1)
        out_ref[m] = lags * scale

    def sent(i, carry):
        block = i // parts
        k = i % parts
        b_core = block % 2
        b_y = (block // 2) % width
        b_z = block // (2 * width)
        straight = (b_core == core) & (b_y == y)

        @pl.when(b_core == core)
        def _():
            copy(block, k, SIB, sibling).wait_send()

        if width > 1:
            @pl.when(straight)
            def _():
                copy(block, k, ACROSS, across).wait_send()

        @pl.when(straight & has_up & (b_z <= z))
        def _():
            copy(block, k, UP, up).wait_send()

        @pl.when(straight & has_down & (b_z >= z))
        def _():
            copy(block, k, DOWN, down).wait_send()

        return carry

    lax.fori_loop(0, blocks * parts, sent, 0)


def per_device(width, noise_window, fir_taps, matchings, block_device):
    rows, total = noise_window.shape
    matches, blocks = matchings.shape
    tiles = total // LAGS
    part = 8 if rows % 8 == 0 else rows
    parts = rows // part
    return pl.pallas_call(
        functools.partial(kernel, width, part),
        out_shape=jax.ShapeDtypeStruct((matches, rows, LAGS), F32),
        in_specs=[pl.BlockSpec(memory_space=pl.ANY)] * 4,
        out_specs=pl.BlockSpec(memory_space=pltpu.VMEM),
        scratch_shapes=[
            pltpu.VMEM((rows, total), F32),
            pltpu.VMEM(fir_taps.shape, F32),
            pltpu.SMEM(matchings.shape, jnp.int32),
            pltpu.SMEM(block_device.shape, jnp.int32),
            pltpu.VMEM((part * (tiles + 8), LAGS), F32),
            pltpu.VMEM((part * (tiles + 8), LAGS), F32),
            pltpu.VMEM((blocks, parts, part * tiles, LAGS), BF16),
            pltpu.VMEM((parts, part * tiles, LAGS), BF16),
            pltpu.VMEM((matches * rows * 8, LAGS), F32),
            pltpu.SemaphoreType.DMA((3 + parts,)),
            pltpu.SemaphoreType.DMA((4, blocks, parts)),
            pltpu.SemaphoreType.DMA((blocks, parts)),
        ],
        compiler_params=pltpu.CompilerParams(
            collective_id=0, has_side_effects=True, vmem_limit_bytes=48 * 2**20
        ),
    )(noise_window, fir_taps, matchings, block_device)


def plane_width(mesh):
    line = mesh.devices.reshape(mesh.shape["grp"], -1)[0]
    places = [getattr(d, "coords", None) for d in line]
    if any(p is None for p in places):
        return 1
    width = len({tuple(p[:2]) for p in places})
    return width if width == 2 and len(places) % 4 == 0 else 1


def solution(mesh):
    return jax.shard_map(
        functools.partial(per_device, plane_width(mesh)),
        mesh=mesh,
        in_specs=(P(("grp", "sta"), None), P(("grp", "sta"), None), P(), P()),
        out_specs=P(None, ("grp", "sta"), None),
        check_vma=False,
    )
```

time: 273 us -> 45.1 us (0.17)
  local copies, waits for them, and re-layouts: 141 us -> 3.77 us
  waiting for transfers between devices: 65.9 us -> 0 us
  Pallas kernels: 0 us -> 40.6 us
  matrix products: 38.3 us -> 0 us
  between operations: 13.6 us -> 0.01 us
  starting transfers between devices: 8.72 us -> 0 us
  other arithmetic: 4.94 us -> 0 us
    gather x6 -> x0, local copies, waits for them, and re-layouts: 137 us -> none  [the longest x2 120 us: whiten(): table = padded[:, position]]
    reduce_scatter x1 -> x0, waiting for transfers between devices: 57.3 us -> none  [per_device(): lax.psum_scatter(partial_sums, 'sta', scatter_dimension=1, tiled=True)]
    pallas_call x0 -> x1, Pallas kernels: none -> 40.6 us  [per_device(): pl.pallas_call(functools.partial(kernel, width, part), out_shape=jax.Shap...]
    another operation x1 -> x0, matrix products: 34.1 us -> none
    all_to_all x1 -> x0, waiting for transfers between devices: 8.61 us -> none  [per_device(): lax.all_to_all(squashed, 'sta', split_axis=1, concat_axis=0, tiled=True)]
    all_to_all x1 -> x0, starting transfers between devices: 7.39 us -> none  [per_device(): lax.all_to_all(squashed, 'sta', split_axis=1, concat_axis=0, tiled=True)]
    dot_general x1 -> x0, matrix products: 4.21 us -> none  [whiten(): jnp.einsum('rkj,rjo->rko', joined, table, precision=lax.Precision.HIGHEST)]
    unnamed x9, local copies, waits for them, and re-layouts: 0.97 us -> 3.77 us
  transfers between devices with their start and end apart: 3 -> 0, of which waited for: 2 -> 0; matrix products, arithmetic and copies ran while one was open for 5% -> 0% of each run, Pallas kernels for 0% -> 0%
where the time goes in v2:
time: 45.1 us; the launch traced here: 44.4 us
  Pallas kernels  40.6 us (90%)
  local copies, waits for them, and re-layouts  3.77 us (8%)
    pallas_call x1, Pallas kernels, per_device(): pl.pallas_call(functools.partial(kernel, width, part), out_shape=jax.Shap...  40.6 us
    unnamed x9, local copies, waits for them, and re-layouts  3.77 us

profile of v2, /device:TPU:0, one launch (start us, length us, event | category | flops | bytes accessed | tf_op | source)
XLA Modules:
  0.0 44.4 jit_solution(17532775453273308299)
XLA Ops:
  0.0 0.0 copy-start
  0.0 1.0 %copy-done = f32[32,4096]{1,0:T(8,128)S(1)} copy-done((f32[32,4096]{1,0:T(8,128)S(1)}, f32[32,4096]{1,0:T(8,128)}, u32[]{:S(2)}) %copy-start) | copy-done | bytes 524312
  1.0 0.0 copy-start.1
  1.0 0.8 %copy-done.1 = f32[32,129]{1,0:T(8,128)S(1)} copy-done((f32[32,129]{1,0:T(8,128)S(1)}, f32[32,129]{1,0:T(8,128)}, u32[]{:S(2)}) %copy-start.1) | copy-done | bytes 16536
  1.8 0.0 copy-start.2
  1.8 0.7 %copy-done.2 = s32[4,16]{1,0:T(4,128)S(1)} copy-done((s32[4,16]{1,0:T(4,128)S(1)}, s32[4,16]{1,0:T(4,128)}, u32[]{:S(2)}) %copy-start.2) | copy-done | bytes 280
  2.5 0.0 copy-start.3
  2.5 0.7 %copy-done.3 = s32[16]{0:T(128)S(1)} copy-done((s32[16]{0:T(128)S(1)}, s32[16]{0:T(128)}, u32[]{:S(2)}) %copy-start.3) | copy-done | bytes 88
  3.1 40.6 %shard_map.46 = f32[4,32,128]{2,1,0:T(8,128)S(1)} custom-call(f32[32,4096]{1,0:T(8,128)S(1)} %copy-done, f32[32,129]{1,0:T(8,128)S(1)} %copy-done.1, s32[4,16]{1,0:T(4,128)S(1)} %copy-done.2, s32[16]{0:T(128)S(1)} %copy-done.3), custom_call_target="tpu_custom_call" | custom-call | tf_op jit(solution)/shard_map/pallas_call | solution.py:261
  43.8 0.6 %copy.6 = f32[4,32,128]{2,1,0:T(8,128)} copy(f32[4,32,128]{2,1,0:T(8,128)S(1)} %shard_map.46) | data formatting | bytes 131072
Async XLA Ops:
  0.0 1.0 %copy-start = (f32[32,4096]{1,0:T(8,128)S(1)}, f32[32,4096]{1,0:T(8,128)}, u32[]{:S(2)}) copy-start(f32[32,4096]{1,0:T(8,128)} %noise_ref.1) | copy-start | bytes 1572868
  1.0 0.8 %copy-start.1 = (f32[32,129]{1,0:T(8,128)S(1)}, f32[32,129]{1,0:T(8,128)}, u32[]{:S(2)}) copy-start(f32[32,129]{1,0:T(8,128)} %taps_ref.1) | copy-start | bytes 49540
  1.8 0.7 %copy-start.2 = (s32[4,16]{1,0:T(4,128)S(1)}, s32[4,16]{1,0:T(4,128)}, u32[]{:S(2)}) copy-start(s32[4,16]{1,0:T(4,128)} %matchings_ref.1) | copy-start | bytes 772
  2.5 0.7 %copy-start.3 = (s32[16]{0:T(128)S(1)}, s32[16]{0:T(128)}, u32[]{:S(2)}) copy-start(s32[16]{0:T(128)} %device_ref.1) | copy-start | bytes 196

commit v3 on v2

--- a/solution.py
+++ b/solution.py
@@ -11,6 +11,7 @@
 F32 = jnp.float32
 BF16 = jnp.bfloat16
 SIB, ACROSS, DOWN, UP = range(4)
+UNROLL = 4
 
 
 def split_bf16(x):
@@ -20,9 +21,10 @@
 
 
 def kernel(width, part, noise_ref, taps_ref, matchings_ref, device_ref, out_ref,
-           noise, taps, matchings, device, xs, ys, gathered, before, acc,
-           in_sems, send_sems, recv_sems):
-    blocks, parts, chunk, _ = gathered.shape
+           noise, taps, matchings, device, xs, ys, own, before, acc,
+           in_sems, send_sems, recv_sems, *gathered):
+    parts = len(gathered)
+    blocks = gathered[0].shape[0]
     rows, total = noise.shape
     matches = matchings.shape[0]
     tiles = total // LAGS
@@ -69,8 +71,8 @@
 
     def copy(block, k, way, target):
         return pltpu.make_async_remote_copy(
-            src_ref=gathered.at[block, k],
-            dst_ref=gathered.at[block, k],
+            src_ref=gathered[k].at[block],
+            dst_ref=gathered[k].at[block],
             send_sem=send_sems.at[way, block, k],
             recv_sem=recv_sems.at[block, k],
             device_id={"sta": target},
@@ -113,7 +115,7 @@
             white = four[:tiles, :LAGS] + (four[tiles:, :LAGS] + four[:tiles, LAGS:] + four[tiles:, LAGS:])
             squashed = white / (1.0 + jnp.abs(white))
             ys[pl.ds(r * pitch + 8, tiles), :] = squashed
-            gathered[me, k, pl.ds(r * tiles, tiles), :] = squashed.astype(BF16)
+            own[k, pl.ds(r * tiles, tiles), :] = squashed.astype(BF16)
             shifted = ys[pl.ds(r * pitch + 7, tiles), :]
             before[k, pl.ds(r * tiles, tiles), :] = shifted.astype(BF16)
 
@@ -121,53 +123,73 @@
         def _():
             pl.semaphore_wait(barrier, 1 + (width > 1) + has_down.astype(jnp.int32) + has_up.astype(jnp.int32))
 
-        if width > 1:
-            copy(me, k, ACROSS, across).start()
-
-        @pl.when(has_down)
-        def _():
-            copy(me, k, DOWN, down).start()
-
-        @pl.when(has_up)
-        def _():
-            copy(me, k, UP, up).start()
-
-        copy(me, k, SIB, sibling).start()
+        for at in range(parts):
+            @pl.when(k == at)
+            def _():
+                gathered[at][me] = own[at]
+                if width > 1:
+                    copy(me, at, ACROSS, across).start()
+
+                @pl.when(has_down)
+                def _():
+                    copy(me, at, DOWN, down).start()
+
+                @pl.when(has_up)
+                def _():
+                    copy(me, at, UP, up).start()
+
+                copy(me, at, SIB, sibling).start()
+
         return carry
 
     lax.fori_loop(0, parts, whiten_part, 0)
+
+    paired = width > 1 and depth % 2 == 0
+    mate = z + 1 - 2 * (z % 2)
+
+    def late(k):
+        return paired and 2 * k >= parts and parts > 1
 
     def along(z_of, way, target, onward, k):
         block = z_of * 2 * width + y * 2 + core
         landed(block, k)
-        if width > 1:
-            copy(block, k, ACROSS, across).start()
 
         @pl.when(onward)
         def _():
             copy(block, k, way, target).start()
 
+        if width > 1:
+            @pl.when(jnp.logical_not(late(k) & (z_of == mate)))
+            def _():
+                copy(block, k, ACROSS, across).start()
+
         copy(block, k, SIB, sibling).start()
 
     def from_across(z_of, k):
         block = z_of * 2 * width + (1 - y) * 2 + core
         landed(block, k)
+        if late(k):
+            @pl.when((z_of == z) & (mate > z))
+            def _():
+                copy(block, k, UP, up).start()
+
+            @pl.when((z_of == z) & (mate < z))
+            def _():
+                copy(block, k, DOWN, down).start()
+
         copy(block, k, SIB, sibling).start()
 
-    def round_part(i, carry):
-        d = i // parts
-        k = i % parts
-
-        @pl.when((d > 0) & (z - d >= 0))
+    def round_part(d, k):
+        @pl.when(z - d >= 0)
         def _():
             along(z - d, UP, up, has_up, k)
 
-        @pl.when((d > 0) & (z + d < depth))
+        @pl.when(z + d < depth)
         def _():
             along(z + d, DOWN, down, has_down, k)
 
         if width > 1:
-            @pl.when((d > 0) & (z - d + 1 >= 0))
+            @pl.when(z - d + 1 >= 0)
             def _():
                 from_across(z - d + 1, k)
 
@@ -175,17 +197,12 @@
             def _():
                 from_across(z + d - 1, k)
 
+    def one_round(d, carry):
+        for k in range(parts):
+            round_part(d, k)
         return carry
 
-    lax.fori_loop(parts, (depth + 1) * parts, round_part, 0)
-
-    def last_part(i, carry):
-        pair = i // parts
-        k = i % parts
-        landed(2 * pair + 1 - core, k)
-        return carry
-
-    lax.fori_loop(0, blocks // 2 * parts, last_part, 0)
+    lax.fori_loop(1, depth, one_round, 0)
 
     partners = []
     mine = device[me]
@@ -196,11 +213,10 @@
             partner = jnp.where(device[e] == wanted, e, partner)
         partners.append(partner)
 
-    def correlate_row(r, carry):
-        k = r // part
-        span = pl.ds(pl.multiple_of((r % part) * tiles, 16), tiles)
-        left = jnp.concatenate([gathered[me, k, span, :], before[k, span, :]], axis=1)
-        right = jnp.concatenate([gathered[partner, k, span, :] for partner in partners], axis=1)
+    def correlate_row(k, r, carry):
+        span = pl.ds(pl.multiple_of(r * tiles, 16), tiles)
+        left = jnp.concatenate([own[k, span, :], before[k, span, :]], axis=1)
+        right = jnp.concatenate([gathered[k][partner, span, :] for partner in partners], axis=1)
         gram = lax.dot_general(left, right, (((0,), (0,)), ((), ())), preferred_element_type=F32)
         for m in range(matches):
             lanes = slice(m * LAGS, (m + 1) * LAGS)
@@ -210,10 +226,22 @@
                 terms.append(pltpu.roll(chosen[g:g + 8], LAGS - g, 1))
             while len(terms) > 1:
                 terms = [a + b for a, b in zip(terms[::2], terms[1::2])]
-            acc[pl.ds(pl.multiple_of((m * rows + r) * 8, 8), 8), :] = terms[0]
+            acc[pl.ds(pl.multiple_of((m * rows + k * part + r) * 8, 8), 8), :] = terms[0]
         return carry
 
-    lax.fori_loop(0, rows, correlate_row, 0, unroll=2)
+    def finish(k):
+        def one(pair, carry):
+            landed(2 * pair + 1 - core, k)
+            return carry
+
+        lax.fori_loop(0, blocks // 2, one, 0)
+        lax.fori_loop(0, part, functools.partial(correlate_row, k), 0, unroll=UNROLL)
+
+    for k in range(parts):
+        round_part(jnp.int32(depth), k)
+        if k > 0:
+            finish(k - 1)
+    finish(parts - 1)
 
     scale = 1.0 / total ** 0.5
     for m in range(matches):
@@ -222,34 +250,35 @@
             lags += pltpu.roll(acc[pl.ds(m * rows * 8 + s, rows, stride=8), :], LAGS - s, 1)
         out_ref[m] = lags * scale
 
-    def sent(i, carry):
-        block = i // parts
-        k = i % parts
+    def sent(block, carry):
         b_core = block % 2
         b_y = (block // 2) % width
         b_z = block // (2 * width)
         straight = (b_core == core) & (b_y == y)
-
-        @pl.when(b_core == core)
-        def _():
-            copy(block, k, SIB, sibling).wait_send()
-
-        if width > 1:
-            @pl.when(straight)
-            def _():
-                copy(block, k, ACROSS, across).wait_send()
-
-        @pl.when(straight & has_up & (b_z <= z))
-        def _():
-            copy(block, k, UP, up).wait_send()
-
-        @pl.when(straight & has_down & (b_z >= z))
-        def _():
-            copy(block, k, DOWN, down).wait_send()
+        for k in range(parts):
+            @pl.when(b_core == core)
+            def _():
+                copy(block, k, SIB, sibling).wait_send()
+
+            turned = jnp.bool_(False)
+            if late(k):
+                turned = (b_core == core) & (b_y != y) & (b_z == z)
+            if width > 1:
+                @pl.when(straight & jnp.logical_not(late(k) & (b_z == mate)))
+                def _():
+                    copy(block, k, ACROSS, across).wait_send()
+
+            @pl.when((straight & has_up & (b_z <= z)) | (turned & (mate > z)))
+            def _():
+                copy(block, k, UP, up).wait_send()
+
+            @pl.when((straight & has_down & (b_z >= z)) | (turned & (mate < z)))
+            def _():
+                copy(block, k, DOWN, down).wait_send()
 
         return carry
 
-    lax.fori_loop(0, blocks * parts, sent, 0)
+    lax.fori_loop(0, blocks, sent, 0)
 
 
 def per_device(width, noise_window, fir_taps, matchings, block_device):
@@ -261,7 +290,7 @@
     return pl.pallas_call(
         functools.partial(kernel, width, part),
         out_shape=jax.ShapeDtypeStruct((matches, rows, LAGS), F32),
-        in_specs=[pl.BlockSpec(memory_space=pl.ANY)] * 4,
+        in_specs=[pl.BlockSpec(memory_space=pltpu.HBM)] * 4,
         out_specs=pl.BlockSpec(memory_space=pltpu.VMEM),
         scratch_shapes=[
             pltpu.VMEM((rows, total), F32),
@@ -270,13 +299,13 @@
             pltpu.SMEM(block_device.shape, jnp.int32),
             pltpu.VMEM((part * (tiles + 8), LAGS), F32),
             pltpu.VMEM((part * (tiles + 8), LAGS), F32),
-            pltpu.VMEM((blocks, parts, part * tiles, LAGS), BF16),
+            pltpu.VMEM((parts, part * tiles, LAGS), BF16),
             pltpu.VMEM((parts, part * tiles, LAGS), BF16),
             pltpu.VMEM((matches * rows * 8, LAGS), F32),
             pltpu.SemaphoreType.DMA((3 + parts,)),
             pltpu.SemaphoreType.DMA((4, blocks, parts)),
             pltpu.SemaphoreType.DMA((blocks, parts)),
-        ],
+        ] + [pltpu.VMEM((blocks, part * tiles, LAGS), BF16)] * parts,
         compiler_params=pltpu.CompilerParams(
             collective_id=0, has_side_effects=True, vmem_limit_bytes=48 * 2**20
         ),

time: 45.1 us -> 41.2 us (0.914)
  Pallas kernels: 40.6 us -> 37.2 us
    pallas_call x1, Pallas kernels: 40.6 us -> 37.2 us  [per_device(): pl.pallas_call(functools.partial(kernel, width, part), out_shape=jax.Shap...]
where the time goes in v3:
time: 41.2 us; the launch traced here: 40.9 us
  Pallas kernels  37.2 us (90%)
  local copies, waits for them, and re-layouts  3.77 us (9%)
    pallas_call x1, Pallas kernels, per_device(): pl.pallas_call(functools.partial(kernel, width, part), out_shape=jax.Shap...  37.2 us
    unnamed x9, local copies, waits for them, and re-layouts  3.77 us

profile of v3, /device:TPU:0, one launch (start us, length us, event | category | flops | bytes accessed | tf_op | source)
XLA Modules:
  0.0 40.9 jit_solution(7127441160925079111)
XLA Ops:
  0.0 0.0 copy-start
  0.0 1.0 %copy-done = f32[32,4096]{1,0:T(8,128)S(1)} copy-done((f32[32,4096]{1,0:T(8,128)S(1)}, f32[32,4096]{1,0:T(8,128)}, u32[]{:S(2)}) %copy-start) | copy-done | bytes 524312
  1.0 0.0 copy-start.1
  1.0 0.8 %copy-done.1 = f32[32,129]{1,0:T(8,128)S(1)} copy-done((f32[32,129]{1,0:T(8,128)S(1)}, f32[32,129]{1,0:T(8,128)}, u32[]{:S(2)}) %copy-start.1) | copy-done | bytes 16536
  1.8 0.0 copy-start.2
  1.8 0.7 %copy-done.2 = s32[4,16]{1,0:T(4,128)S(1)} copy-done((s32[4,16]{1,0:T(4,128)S(1)}, s32[4,16]{1,0:T(4,128)}, u32[]{:S(2)}) %copy-start.2) | copy-done | bytes 280
  2.5 0.0 copy-start.3
  2.5 0.7 %copy-done.3 = s32[16]{0:T(128)S(1)} copy-done((s32[16]{0:T(128)S(1)}, s32[16]{0:T(128)}, u32[]{:S(2)}) %copy-start.3) | copy-done | bytes 88
  3.1 37.2 %shard_map.46 = f32[4,32,128]{2,1,0:T(8,128)S(1)} custom-call(f32[32,4096]{1,0:T(8,128)S(1)} %copy-done, f32[32,129]{1,0:T(8,128)S(1)} %copy-done.1, s32[4,16]{1,0:T(4,128)S(1)} %copy-done.2, s32[16]{0:T(128)S(1)} %copy-done.3), custom_call_target="tpu_custom_call" | custom-call | tf_op jit(solution)/shard_map/pallas_call | solution.py:290
  40.3 0.6 %copy.6 = f32[4,32,128]{2,1,0:T(8,128)} copy(f32[4,32,128]{2,1,0:T(8,128)S(1)} %shard_map.46) | data formatting | bytes 131072
Async XLA Ops:
  0.0 1.0 %copy-start = (f32[32,4096]{1,0:T(8,128)S(1)}, f32[32,4096]{1,0:T(8,128)}, u32[]{:S(2)}) copy-start(f32[32,4096]{1,0:T(8,128)} %noise_ref.1) | copy-start | bytes 1572868
  1.0 0.8 %copy-start.1 = (f32[32,129]{1,0:T(8,128)S(1)}, f32[32,129]{1,0:T(8,128)}, u32[]{:S(2)}) copy-start(f32[32,129]{1,0:T(8,128)} %taps_ref.1) | copy-start | bytes 49540
  1.8 0.7 %copy-start.2 = (s32[4,16]{1,0:T(4,128)S(1)}, s32[4,16]{1,0:T(4,128)}, u32[]{:S(2)}) copy-start(s32[4,16]{1,0:T(4,128)} %matchings_ref.1) | copy-start | bytes 772
  2.5 0.7 %copy-start.3 = (s32[16]{0:T(128)S(1)}, s32[16]{0:T(128)}, u32[]{:S(2)}) copy-start(s32[16]{0:T(128)} %device_ref.1) | copy-start | bytes 196

commit v4 on v3

--- a/solution.py
+++ b/solution.py
@@ -139,10 +139,10 @@
                     copy(me, at, UP, up).start()
 
                 copy(me, at, SIB, sibling).start()
+                if at >= 2 and depth > 1:
+                    round_part(jnp.int32(1), at - 2)
 
         return carry
-
-    lax.fori_loop(0, parts, whiten_part, 0)
 
     paired = width > 1 and depth % 2 == 0
     mate = z + 1 - 2 * (z % 2)
@@ -202,7 +202,12 @@
             round_part(d, k)
         return carry
 
-    lax.fori_loop(1, depth, one_round, 0)
+    lax.fori_loop(0, parts, whiten_part, 0)
+
+    if depth > 1:
+        for k in range(max(parts - 2, 0), parts):
+            round_part(jnp.int32(1), k)
+        lax.fori_loop(2, depth, one_round, 0)
 
     partners = []
     mine = device[me]

time: 41.2 us -> 40.9 us (level)
  no operation moved by 1% of the time
where the time goes in v4:
time: 40.9 us; the launch traced here: 40.7 us
  Pallas kernels  36.9 us (90%)
  local copies, waits for them, and re-layouts  3.77 us (9%)
    pallas_call x1, Pallas kernels, per_device(): pl.pallas_call(functools.partial(kernel, width, part), out_shape=jax.Shap...  36.9 us
    unnamed x9, local copies, waits for them, and re-layouts  3.77 us

profile of v4, /device:TPU:0, one launch (start us, length us, event | category | flops | bytes accessed | tf_op | source)
XLA Modules:
  0.0 40.7 jit_solution(15369690683551031358)
XLA Ops:
  0.0 0.0 copy-start
  0.0 1.0 %copy-done = f32[32,4096]{1,0:T(8,128)S(1)} copy-done((f32[32,4096]{1,0:T(8,128)S(1)}, f32[32,4096]{1,0:T(8,128)}, u32[]{:S(2)}) %copy-start) | copy-done | bytes 524312
  1.0 0.0 copy-start.1
  1.0 0.8 %copy-done.1 = f32[32,129]{1,0:T(8,128)S(1)} copy-done((f32[32,129]{1,0:T(8,128)S(1)}, f32[32,129]{1,0:T(8,128)}, u32[]{:S(2)}) %copy-start.1) | copy-done | bytes 16536
  1.8 0.0 copy-start.2
  1.8 0.7 %copy-done.2 = s32[4,16]{1,0:T(4,128)S(1)} copy-done((s32[4,16]{1,0:T(4,128)S(1)}, s32[4,16]{1,0:T(4,128)}, u32[]{:S(2)}) %copy-start.2) | copy-done | bytes 280
  2.5 0.0 copy-start.3
  2.5 0.7 %copy-done.3 = s32[16]{0:T(128)S(1)} copy-done((s32[16]{0:T(128)S(1)}, s32[16]{0:T(128)}, u32[]{:S(2)}) %copy-start.3) | copy-done | bytes 88
  3.1 36.9 %shard_map.46 = f32[4,32,128]{2,1,0:T(8,128)S(1)} custom-call(f32[32,4096]{1,0:T(8,128)S(1)} %copy-done, f32[32,129]{1,0:T(8,128)S(1)} %copy-done.1, s32[4,16]{1,0:T(4,128)S(1)} %copy-done.2, s32[16]{0:T(128)S(1)} %copy-done.3), custom_call_target="tpu_custom_call" | custom-call | tf_op jit(solution)/shard_map/pallas_call | solution.py:295
  40.0 0.6 %copy.6 = f32[4,32,128]{2,1,0:T(8,128)} copy(f32[4,32,128]{2,1,0:T(8,128)S(1)} %shard_map.46) | data formatting | bytes 131072
Async XLA Ops:
  0.0 1.0 %copy-start = (f32[32,4096]{1,0:T(8,128)S(1)}, f32[32,4096]{1,0:T(8,128)}, u32[]{:S(2)}) copy-start(f32[32,4096]{1,0:T(8,128)} %noise_ref.1) | copy-start | bytes 1572868
  1.0 0.8 %copy-start.1 = (f32[32,129]{1,0:T(8,128)S(1)}, f32[32,129]{1,0:T(8,128)}, u32[]{:S(2)}) copy-start(f32[32,129]{1,0:T(8,128)} %taps_ref.1) | copy-start | bytes 49540
  1.8 0.7 %copy-start.2 = (s32[4,16]{1,0:T(4,128)S(1)}, s32[4,16]{1,0:T(4,128)}, u32[]{:S(2)}) copy-start(s32[4,16]{1,0:T(4,128)} %matchings_ref.1) | copy-start | bytes 772
  2.5 0.7 %copy-start.3 = (s32[16]{0:T(128)S(1)}, s32[16]{0:T(128)}, u32[]{:S(2)}) copy-start(s32[16]{0:T(128)} %device_ref.1) | copy-start | bytes 196

commit v5 on v4

--- a/solution.py
+++ b/solution.py
@@ -11,7 +11,7 @@
 F32 = jnp.float32
 BF16 = jnp.bfloat16
 SIB, ACROSS, DOWN, UP = range(4)
-UNROLL = 4
+UNROLL = 8
 
 
 def split_bf16(x):
@@ -148,7 +148,7 @@
     mate = z + 1 - 2 * (z % 2)
 
     def late(k):
-        return paired and 2 * k >= parts and parts > 1
+        return paired and 4 * k >= 3 * parts and parts > 1
 
     def along(z_of, way, target, onward, k):
         block = z_of * 2 * width + y * 2 + core

time: 40.9 us -> 38.4 us (0.939)
  Pallas kernels: 36.9 us -> 34.3 us
    pallas_call x1, Pallas kernels: 36.9 us -> 34.3 us  [per_device(): pl.pallas_call(functools.partial(kernel, width, part), out_shape=jax.Shap...]
where the time goes in v5:
time: 38.4 us; the launch traced here: 38.1 us
  Pallas kernels  34.3 us (89%)
  local copies, waits for them, and re-layouts  3.77 us (10%)
    pallas_call x1, Pallas kernels, per_device(): pl.pallas_call(functools.partial(kernel, width, part), out_shape=jax.Shap...  34.3 us
    unnamed x9, local copies, waits for them, and re-layouts  3.77 us

profile of v5, /device:TPU:0, one launch (start us, length us, event | category | flops | bytes accessed | tf_op | source)
XLA Modules:
  0.0 38.1 jit_solution(14773800062017113001)
XLA Ops:
  0.0 0.0 copy-start
  0.0 1.0 %copy-done = f32[32,4096]{1,0:T(8,128)S(1)} copy-done((f32[32,4096]{1,0:T(8,128)S(1)}, f32[32,4096]{1,0:T(8,128)}, u32[]{:S(2)}) %copy-start) | copy-done | bytes 524312
  1.0 0.0 copy-start.1
  1.0 0.8 %copy-done.1 = f32[32,129]{1,0:T(8,128)S(1)} copy-done((f32[32,129]{1,0:T(8,128)S(1)}, f32[32,129]{1,0:T(8,128)}, u32[]{:S(2)}) %copy-start.1) | copy-done | bytes 16536
  1.8 0.0 copy-start.2
  1.8 0.7 %copy-done.2 = s32[4,16]{1,0:T(4,128)S(1)} copy-done((s32[4,16]{1,0:T(4,128)S(1)}, s32[4,16]{1,0:T(4,128)}, u32[]{:S(2)}) %copy-start.2) | copy-done | bytes 280
  2.5 0.0 copy-start.3
  2.5 0.7 %copy-done.3 = s32[16]{0:T(128)S(1)} copy-done((s32[16]{0:T(128)S(1)}, s32[16]{0:T(128)}, u32[]{:S(2)}) %copy-start.3) | copy-done | bytes 88
  3.1 34.3 %shard_map.46 = f32[4,32,128]{2,1,0:T(8,128)S(1)} custom-call(f32[32,4096]{1,0:T(8,128)S(1)} %copy-done, f32[32,129]{1,0:T(8,128)S(1)} %copy-done.1, s32[4,16]{1,0:T(4,128)S(1)} %copy-done.2, s32[16]{0:T(128)S(1)} %copy-done.3), custom_call_target="tpu_custom_call" | custom-call | tf_op jit(solution)/shard_map/pallas_call | solution.py:295
  37.5 0.6 %copy.6 = f32[4,32,128]{2,1,0:T(8,128)} copy(f32[4,32,128]{2,1,0:T(8,128)S(1)} %shard_map.46) | data formatting | bytes 131072
Async XLA Ops:
  0.0 1.0 %copy-start = (f32[32,4096]{1,0:T(8,128)S(1)}, f32[32,4096]{1,0:T(8,128)}, u32[]{:S(2)}) copy-start(f32[32,4096]{1,0:T(8,128)} %noise_ref.1) | copy-start | bytes 1572868
  1.0 0.8 %copy-start.1 = (f32[32,129]{1,0:T(8,128)S(1)}, f32[32,129]{1,0:T(8,128)}, u32[]{:S(2)}) copy-start(f32[32,129]{1,0:T(8,128)} %taps_ref.1) | copy-start | bytes 49540
  1.8 0.7 %copy-start.2 = (s32[4,16]{1,0:T(4,128)S(1)}, s32[4,16]{1,0:T(4,128)}, u32[]{:S(2)}) copy-start(s32[4,16]{1,0:T(4,128)} %matchings_ref.1) | copy-start | bytes 772
  2.5 0.7 %copy-start.3 = (s32[16]{0:T(128)S(1)}, s32[16]{0:T(128)}, u32[]{:S(2)}) copy-start(s32[16]{0:T(128)} %device_ref.1) | copy-start | bytes 196
